TPU v7x, 32 devices: a whole 2x2x4 slice. The times are simulated.
32 devices in a mesh: gx: 4 (over z), gy: 8 (over y, x, core).
Axes of the slice: x: 2, y: 2, z: 4, core: 2. Of those that a mesh axis runs over, the one named last changes fastest.
Arguments:
- initial_guess: float32 [5, 32, 256, 128], P(None, 'gx', 'gy'), may hold values from -6 to 6
- right_side: float32 [5, 32, 256, 128], P(None, 'gx', 'gy'), may hold values from -6 to 6
- coefficients: float32 [5, 32, 256, 128], P(None, 'gx', 'gy'), may hold values from 0.3 to 3
- tunnel_mask: int32 [32, 256, 128], P('gx', 'gy'), may hold values 0 or 1
- stencil: float32 [27, 5, 5], replicated, may hold values from -0.03 to 1.15, as said below
Outputs:
- fine_iterate: float32 [5, 32, 256, 128], P(None, 'gx', 'gy')
- middle_iterate: float32 [5, 16, 128, 128], P(None, 'gx', 'gy')
- lower_iterate: float32 [5, 8, 64, 128], P(None, 'gx', 'gy')
- coarse_residual: float32 [5, 4, 32, 128], P(None, 'gx', 'gy')
Inputs may be any that keep to these rules, and one draw needn't show every extreme that they name: `stencil`: entries of all 27 blocks; the centre block's diagonal lies in 0.85 to 1.15; off-centre blocks have diagonal entries in -0.025 to -0.01 and off-diagonal entries in -0.004 to 0.004; the centre block's off-diagonal entries lie in -0.02 to 0.02.
All inputs are finite; a program needn't handle non-finite values. No bound on the sum of `tunnel_mask` on one device may be relied on, other than what follows from the above.
Results may differ from a plain program's by a relative error of at most 0.00029.
Values sent between devices are 32-bit elements; how exact they have to be, the bound alone decides.
A program may use at most 64 MiB of HBM per device.

v0:
```python
import functools

import jax
import jax.numpy as jnp
import numpy as np
from jax import lax
from jax.experimental import pallas as pl
from jax.experimental.pallas import tpu as pltpu
from jax.sharding import PartitionSpec as P

MESH = pl.DeviceIdType.MESH
COMP = 5
DAMPING = 0.7
WEIGHTS = (0.125, 0.375, 0.375, 0.125)
LEVELS = 4
ROUNDS = (4, 3, 3, 2)
DIRECTIONS = [(dx, dy) for dx in (-1, 0, 1) for dy in (-1, 0, 1) if (dx, dy) != (0, 0)]
FAR = [(dx, dy) for dx in (-2, 2) for dy in (-1, 0, 1)]
ALL = DIRECTIONS + FAR
FACES_Y = [i for i, d in enumerate(DIRECTIONS) if d[0] == 0]
FACES_X = [i for i, d in enumerate(DIRECTIONS) if d[0] != 0]
F32, BF16 = jnp.float32, jnp.bfloat16


class Level:
    def __init__(self, extent_x, extent_y, ring, at):
        self.x, self.y, self.ring = extent_x, extent_y, ring
        self.yp = max(8, extent_y)
        self.rows = -(-COMP * self.yp // 16) * 16
        self.depth = self.rows + (32 if ring else 16)
        self.out = self.rows + (16 if ring else 0)
        self.halo = self.depth - self.rows
        pos = np.full((self.depth,), -100, np.int32)
        unknown = np.zeros((self.depth,), np.int32)
        for b in range(COMP):
            pos[b * self.yp : b * self.yp + self.y] = np.arange(self.y)
            unknown[b * self.yp : (b + 1) * self.yp] = b
            for i, y in enumerate((-1, self.y, -2, self.y + 1)[: self.halo // 8]):
                pos[self.rows + 8 * i + b], unknown[self.rows + 8 * i + b] = y, b
        self.total = 9 * self.depth
        self.at = at
        self.end = at + -(-self.total // 128) * 128
        hot = np.zeros((15, 3 * self.depth), np.float32)
        for ox in range(3):
            hot[ox * COMP + unknown, ox * self.depth + np.arange(self.depth)] = 1.0
        self.plan = np.zeros((16, self.end - at), np.float32)
        self.plan[:15, : self.total] = np.tile(hot, (1, 3))
        self.plan[15, : self.total] = np.tile(pos, 9)


def transfer_matrices(fine, coarse):
    restrict = np.zeros((coarse.rows, fine.rows + 16), np.float32)
    mean = np.zeros((coarse.rows, fine.rows), np.float32)
    for a in range(COMP):
        for j in range(coarse.y):
            row = a * coarse.yp + j
            for t in range(4):
                y = 2 * j - 1 + t
                if y < 0:
                    column = fine.rows + a
                elif y >= fine.y:
                    column = fine.rows + 8 + a
                else:
                    column = a * fine.yp + y
                restrict[row, column] = WEIGHTS[t]
            mean[row, a * fine.yp + 2 * j] = 0.5
            mean[row, a * fine.yp + 2 * j + 1] = 0.5
    return np.tile(restrict, (1, 2)), np.tile(mean, (1, 2))


def split(values):
    high = values.astype(BF16)
    return high, (values - high.astype(F32)).astype(BF16)


def kernel(levels, count_x, count_y, *refs):
    refs = list(refs)
    take = lambda n: [refs.pop(0) for _ in range(n)]
    guess_ref, right_ref, conduct_ref, mask_ref, stencil_ref, plan_ref, moves_ref = take(7)
    outs = take(4)
    weight = take(LEVELS)
    high, low = take(LEVELS), take(LEVELS)
    high2, low2 = take(LEVELS), take(LEVELS)
    conduct, share, force, ratio, gain, state = [take(LEVELS) for _ in range(6)]
    edge, side, side_out = [take(sum(ROUNDS)) for _ in range(3)]
    send_sem, recv_sem = take(2)

    at_x, at_y = lax.axis_index("gx"), lax.axis_index("gy")

    def inside(dx, dy):
        okay = None
        for shift, at, count in ((dx, at_x, count_x), (dy, at_y, count_y)):
            if shift:
                here = at >= -shift if shift < 0 else at < count - shift
                okay = here if okay is None else jnp.logical_and(okay, here)
        return okay

    first_round = [sum(ROUNDS[:l]) for l in range(LEVELS)]

    def width_of(rnd):
        return 2 if any(rnd == first_round[l] + 1 for l in range(1, LEVELS)) else 1

    def ways(l, rnd):
        return range(len(ALL) if levels[l].x == 1 and width_of(rnd) == 2 else len(DIRECTIONS))

    for l, lev in enumerate(levels):
        for rnd in range(first_round[l], first_round[l] + ROUNDS[l]):
            width = width_of(rnd)
            edge[rnd][pl.ds(0, width)] = jnp.zeros((width, lev.rows, 128), F32)
            edge[rnd][pl.ds(lev.x + width, width)] = jnp.zeros((width, lev.rows, 128), F32)
            side[rnd][...] = jnp.zeros(side[rnd].shape, F32)
            side_out[rnd][...] = jnp.zeros(side_out[rnd].shape, F32)

    barrier = pltpu.get_barrier_semaphore()
    for dx, dy in ALL:
        @pl.when(inside(dx, dy))
        def _(dx=dx, dy=dy):
            pl.semaphore_signal(barrier, inc=1, device_id=(at_x + dx, at_y + dy), device_id_type=MESH)

    def span(at, count, reach):
        total = 1
        for shift in range(1, reach + 1):
            total = total + jnp.where(at >= shift, 1, 0) + jnp.where(at < count - shift, 1, 0)
        return total

    neighbours = span(at_x, count_x, 2) * span(at_y, count_y, 1) - 1

    def copy(l, rnd, index):
        lev, width = levels[l], width_of(rnd)
        dx, dy = ALL[index]
        if lev.x >= width:
            mine, theirs, n = (lev.x - width if dx > 0 else 0), (0 if dx > 0 else lev.x + width), width
        else:
            mine, theirs, n = 0, width - dx, 1
        if dx == 0:
            mine, theirs, n = 0, width, lev.x
        if dy == 0:
            src, dst = edge[rnd].at[pl.ds(width + mine, n)], edge[rnd].at[pl.ds(theirs, n)]
        else:
            out_at, in_at = (1, 0) if dy > 0 else (0, 1)
            src = side_out[rnd].at[out_at, pl.ds(mine, n)]
            dst = side[rnd].at[in_at, pl.ds(theirs, n)]
        return pltpu.make_async_remote_copy(
            src_ref=src,
            dst_ref=dst,
            send_sem=send_sem.at[rnd, index],
            recv_sem=recv_sem.at[rnd, index],
            device_id=(at_x + dx, at_y + dy),
            device_id_type=MESH,
        )

    def send(l, rnd):
        for index in [i for i in ways(l, rnd) if i not in FACES_Y] + FACES_Y:
            @pl.when(inside(*ALL[index]))
            def _(index=index):
                copy(l, rnd, index).start()

    def receive(l, rnd, which):
        for index in which:
            dx, dy = ALL[index]
            @pl.when(inside(-dx, -dy))
            def _(index=index):
                copy(l, rnd, index).wait_recv()

    def finish(l, rnd):
        for index in ways(l, rnd):
            @pl.when(inside(*ALL[index]))
            def _(index=index):
                copy(l, rnd, index).wait_send()

    def put(l, rnd, x, values):
        lev, width = levels[l], width_of(rnd)
        edge[rnd][x + width] = values
        for b in range(COMP):
            for i in range(width):
                y = b * lev.yp + i
                side_out[rnd][0, x, pl.ds(8 * i + b, 1), :] = values[y : y + 1]
                y = b * lev.yp + lev.y - 1 - i
                side_out[rnd][1, x, pl.ds(8 * i + b, 1), :] = values[y : y + 1]

    def convert(l, rnd, x):
        lev = levels[l]
        halo = [side[rnd][i, x, pl.ds(k, 8), :] for k in range(0, lev.halo // 2, 8) for i in range(2)]
        for start, values in ((0, edge[rnd][x]), (lev.rows, jnp.concatenate(halo, axis=0))):
            a, b = split(values)
            high[l][x, pl.ds(start, values.shape[0]), :] = a
            low[l][x, pl.ds(start, values.shape[0]), :] = b

    def apply_group(l, x0, n, high_ref, low_ref):
        lev = levels[l]
        halves = []
        for i in range(n):
            a = high_ref[pl.ds(x0 + i, 3)].reshape(3 * lev.depth, 128)
            b = low_ref[pl.ds(x0 + i, 3)].reshape(3 * lev.depth, 128)
            halves.append(jnp.concatenate([a, a, b], axis=0))
        rhs = halves[0] if n == 1 else jnp.concatenate(halves, axis=1)
        product = jnp.dot(weight[l][...], rhs, preferred_element_type=F32)
        lane = lax.broadcasted_iota(jnp.int32, (lev.out, 128), 1)
        sums = []
        for i in range(n):
            below, centre, above = [
                product[k * lev.out : (k + 1) * lev.out, i * 128 : (i + 1) * 128] for k in range(3)
            ]
            below = jnp.where(lane == 0, 0.0, pltpu.roll(below, 1, 1))
            above = jnp.where(lane == 127, 0.0, pltpu.roll(above, 127, 1))
            sums.append(centre + below + above)
        return sums

    def sweep_fine(rnd, store):
        lev = levels[0]
        pairs = lev.x // 2

        def pair(p, _):
            for i, summed in enumerate(apply_group(0, 2 * p, 2, high[0], low[0])):
                store(2 * p + i, summed)
            return 0

        receive(0, rnd, FACES_Y)
        lax.fori_loop(1, lev.x + 1, lambda x, _: (convert(0, rnd, x), 0)[1], 0)
        lax.fori_loop(1, pairs - 1, pair, 0)
        receive(0, rnd, FACES_X)
        convert(0, rnd, 0)
        convert(0, rnd, lev.x + 1)
        lax.fori_loop(0, 2, lambda p, _: pair(p * (pairs - 1), 0), 0)

    def build_weight(l):
        lev = levels[l]
        total = lev.total
        segment = pl.ds(lev.at, lev.end - lev.at)
        spread = sum(
            jnp.dot(
                jnp.concatenate([stencil_ref[9 * ox + i] for i in range(9)], axis=0),
                plan_ref[pl.ds(COMP * ox, COMP), segment],
                precision=lax.Precision.HIGHEST,
                preferred_element_type=F32,
            )
            for ox in range(3)
        )[:, :total]
        place = plan_ref[pl.ds(15, 1), segment][:, :total].astype(jnp.int32)
        row = lax.broadcasted_iota(jnp.int32, (lev.yp, total), 0)
        lane = lax.broadcasted_iota(jnp.int32, (lev.out, total), 1)
        pos = jnp.where(row < lev.y, jnp.broadcast_to(place, (lev.yp, total)), -100)
        ring_pos = jnp.broadcast_to(place, (COMP, total))
        bands = [pos == row + oy for oy in (-1, 0, 1)]
        middle = jnp.logical_and(lane >= 3 * lev.depth, lane < 6 * lev.depth)
        for oz in range(3):
            blocks = []
            for a in range(COMP):
                block = jnp.zeros((lev.yp, total), F32)
                for oy in range(3):
                    at = oy * 15 + oz * COMP + a
                    block = jnp.where(bands[oy], spread[at : at + 1, :], block)
                blocks.append(block)
            if lev.rows > COMP * lev.yp:
                blocks.append(jnp.zeros((lev.rows - COMP * lev.yp, total), F32))
            if lev.ring:
                for y in (-1, lev.y):
                    block = jnp.zeros((COMP, total), F32)
                    for oy in range(3):
                        at = oy * 15 + oz * COMP
                        block = jnp.where(ring_pos == y + oy - 1, spread[at : at + COMP, :], block)
                    blocks += [block, jnp.zeros((8 - COMP, total), F32)]
            block = jnp.concatenate(blocks, axis=0)
            upper = block.astype(BF16).astype(F32)
            weight[l][pl.ds(oz * lev.out, lev.out), :] = jnp.where(middle, block - upper, upper).astype(BF16)

    def relax(lev):
        centre = stencil_ref[13]
        pieces = [
            DAMPING / jnp.broadcast_to(centre[a : a + 1, a : a + 1], (lev.yp, 128)) for a in range(COMP)
        ]
        if lev.rows > COMP * lev.yp:
            pieces.append(jnp.zeros((lev.rows - COMP * lev.yp, 128), F32))
        return jnp.concatenate(pieces, axis=0)

    def matrix(l, which):
        fine, lev = levels[l], levels[l + 1]
        at = sum(2 * levels[i + 1].rows for i in range(l)) + which * lev.rows
        return moves_ref[pl.ds(at, lev.rows), pl.ds(0, 2 * (fine.rows + (0 if which else 16)))]

    def coarse_means(l):
        fine, lev = levels[l], levels[l + 1]
        scale = relax(lev)
        for x in range(lev.x):
            if l == 0:
                c = 0.5 * (conduct_ref[:, 2 * x] + conduct_ref[:, 2 * x + 1])
                c = c.reshape(fine.rows, 128)
            else:
                c = 0.5 * (conduct[l][2 * x] + conduct[l][2 * x + 1])
            s = 0.5 * (share[l][2 * x] + share[l][2 * x + 1])
            c2 = jnp.concatenate(split(c), axis=0)
            s2 = jnp.concatenate(split(s), axis=0)
            both = jnp.dot(matrix(l, 1), jnp.concatenate([c2, s2], axis=1), preferred_element_type=F32)
            conduct[l + 1][x] = jnp.maximum(both[:, :128], 0.01)
            share[l + 1][x] = both[:, 128:]
            gain[l + 1][x] = scale * both[:, 128:]
            put(l + 1, first_round[l + 1], x, scale * both[:, 128:] * both[:, 128:])
        send(l + 1, first_round[l + 1])

    def restrict(l, rnd):
        fine, lev = levels[l], levels[l + 1]
        receive(l, rnd, FACES_Y + FACES_X)
        columns = []
        for x in range(lev.x):
            parts = []
            for ref in (edge[rnd], side[rnd].at[0], side[rnd].at[1]):
                parts.append(sum(WEIGHTS[t] * ref[2 * x + t] for t in range(4)))
            columns.append(jnp.concatenate(split(jnp.concatenate(parts, axis=0)), axis=0))
        rhs = columns[0] if lev.x == 1 else jnp.concatenate(columns, axis=1)
        product = jnp.dot(matrix(l, 0), rhs, preferred_element_type=F32)
        nxt = first_round[l + 1] + 1
        for x in range(lev.x):
            f = product[:, x * 128 : (x + 1) * 128]
            force[l + 1][x] = f
            g = f / conduct[l + 1][x]
            v = gain[l + 1][x] * g
            state[l + 1][x] = v
            put(l + 1, nxt, x, share[l + 1][x] * v)
        send(l + 1, nxt)

    fine = levels[0]

    def start(x, _):
        s = mask_ref[x].astype(F32)
        s = jnp.concatenate([s] * COMP, axis=0)
        share[0][x] = s
        put(0, 0, x, s * guess_ref[:, x].reshape(fine.rows, 128))
        return 0

    lax.fori_loop(0, fine.x, start, 0)
    pl.semaphore_wait(barrier, neighbours)
    send(0, 0)

    scale = relax(fine)

    def prepare(x, _):
        f = right_ref[:, x].reshape(fine.rows, 128)
        ratio[0][x] = f / conduct_ref[:, x].reshape(fine.rows, 128)
        gain[0][x] = scale * share[0][x]
        return 0

    lax.fori_loop(0, fine.x, prepare, 0)
    for l in range(LEVELS - 1):
        coarse_means(l)
    for l in range(LEVELS):
        build_weight(l)
    for l in range(1, LEVELS):
        for ref in (high2[l], low2[l]):
            ref[:, pl.ds(levels[l].out, 16), :] = jnp.zeros((levels[l].x + 2, 16, 128), BF16)

    def first(x, summed):
        v = guess_ref[:, x].reshape(fine.rows, 128) + gain[0][x] * (ratio[0][x] - summed)
        state[0][x] = v
        put(0, 1, x, share[0][x] * v)

    def second(x, summed):
        v = state[0][x] + gain[0][x] * (ratio[0][x] - summed)
        outs[0][:, x] = v.reshape(COMP, fine.y, 128)
        put(0, 2, x, share[0][x] * v)

    def third(x, summed):
        f = right_ref[:, x].reshape(fine.rows, 128)
        c = conduct_ref[:, x].reshape(fine.rows, 128)
        put(0, 3, x, share[0][x] * (f - c * summed))

    for rnd, store in enumerate((first, second, third)):
        sweep_fine(rnd, store)
        send(0, rnd + 1)

    for l in range(1, LEVELS):
        lev, base = levels[l], first_round[l]
        restrict(l - 1, base - 1)

        wide = 2 if lev.x > 1 else 3
        receive(l, base + 1, ways(l, base + 1))
        lax.fori_loop(0, lev.x + 4, lambda x, _, l=l, base=base: (convert(l, base + 1, x), 0)[1], 0)
        receive(l, base, FACES_Y + FACES_X)

        def smooth(p, _, l=l, lev=lev, base=base, wide=wide):
            for i, summed in enumerate(apply_group(l, p * wide, wide, high[l], low[l])):
                x = p * wide + i
                m = [edge[base + 1][x + 1]] + [side[base + 1][k, x + 1, pl.ds(0, 8), :] for k in range(2)]
                q = [edge[base][x], side[base][0, x], side[base][1, x]]
                m = 2.0 * jnp.concatenate(m, axis=0) - jnp.concatenate(q, axis=0) * summed
                a, b = split(m)
                high2[l][x, pl.ds(0, lev.out), :] = a
                low2[l][x, pl.ds(0, lev.out), :] = b
                if l < LEVELS - 1:
                    @pl.when(jnp.logical_and(x >= 1, x <= lev.x))
                    def _(summed=summed, x=x):
                        v = 2.0 * state[l][x - 1] - gain[l][x - 1] * summed[: lev.rows]
                        outs[l][:, x - 1] = v[: COMP * lev.yp].reshape(COMP, lev.y, 128)
            return 0

        def remain(p, _, l=l, lev=lev, base=base):
            n = min(2, lev.x)
            for i, summed in enumerate(apply_group(l, p * n, n, high2[l], low2[l])):
                x = p * n + i
                r = share[l][x] * (force[l][x] - conduct[l][x] * summed[: lev.rows])
                if l < LEVELS - 1:
                    put(l, base + 2, x, r)
                else:
                    outs[l][:, x] = r[: COMP * lev.yp].reshape(COMP, lev.yp, 128)[:, : lev.y]
            return 0

        lax.fori_loop(0, (lev.x + 2) // wide, smooth, 0)
        lax.fori_loop(0, max(1, lev.x // 2), remain, 0)
        if l < LEVELS - 1:
            send(l, base + 2)

    for l in range(LEVELS):
        for rnd in range(first_round[l], first_round[l] + ROUNDS[l]):
            finish(l, rnd)


def body(count_x, count_y, initial_guess, right_side, coefficients, tunnel_mask, stencil):
    extent_x, extent_y = initial_guess.shape[1], initial_guess.shape[2]
    levels, at = [], 0
    for l in range(LEVELS):
        levels.append(Level(extent_x >> l, extent_y >> l, l > 0, at))
        at = levels[-1].end
    plan = np.concatenate([lev.plan for lev in levels], axis=1)
    moves = [m for l in range(LEVELS - 1) for m in transfer_matrices(levels[l], levels[l + 1])]
    widest = -(-max(m.shape[1] for m in moves) // 128) * 128
    moves = np.concatenate([np.pad(m, ((0, 0), (0, widest - m.shape[1]))) for m in moves], axis=0)
    operands = [initial_guess, right_side, coefficients, tunnel_mask, stencil]
    operands += [jnp.asarray(plan), jnp.asarray(moves, BF16)]
    vmem = pl.BlockSpec(memory_space=pltpu.VMEM)
    scratch = [pltpu.VMEM((3 * lev.out, lev.total), BF16) for lev in levels]
    for extra in (4, 4, 2, 2):
        scratch += [pltpu.VMEM((lev.x + extra, lev.depth, 128), BF16) for lev in levels]
    for _ in range(6):
        scratch += [pltpu.VMEM((lev.x, lev.rows, 128), F32) for lev in levels]
    of_round = [(lev, 2 if lev.ring and i == 1 else 1) for lev, n in zip(levels, ROUNDS) for i in range(n)]
    scratch += [pltpu.VMEM((lev.x + 2 * width, lev.rows, 128), F32) for lev, width in of_round]
    scratch += [pltpu.VMEM((2, lev.x + 2 * width, 8 * width, 128), F32) for lev, width in of_round]
    scratch += [pltpu.VMEM((2, lev.x, 8 * width, 128), F32) for lev, width in of_round]
    scratch += [pltpu.SemaphoreType.DMA((len(of_round), len(ALL)))] * 2
    return pl.pallas_call(
        functools.partial(kernel, levels, count_x, count_y),
        out_shape=[jax.ShapeDtypeStruct((COMP, lev.x, lev.y, 128), F32) for lev in levels],
        in_specs=[vmem] * len(operands),
        out_specs=[vmem] * 4,
        scratch_shapes=scratch,
        compiler_params=pltpu.CompilerParams(
            collective_id=0, has_side_effects=True, vmem_limit_bytes=48 * 1024 * 1024
        ),
    )(*operands)


def solution(mesh):
    grid = P(None, "gx", "gy", None)
    return jax.shard_map(
        functools.partial(body, mesh.shape["gx"], mesh.shape["gy"]),
        mesh=mesh,
        in_specs=(grid, grid, grid, P("gx", "gy", None), P()),
        out_specs=(grid,) * 4,
        check_vma=False,
    )
```

profile of v0, /device:TPU:4, one launch (start us, length us, event | category | flops | bytes accessed | tf_op | source)
XLA Modules:
  0.0 64.5 jit_solution(9692575298735146465)
XLA Ops:
  0.6 0.0 copy-start.5
  0.6 0.9 %copy.11.refs_4_ = f32[27,5,5]{2,1,0:T(8,128)S(1)} copy(f32[27,5,5]{0,2,1:T(8,128)} %param.11) | data formatting | bytes 5400 | tf_op args[4]
  1.5 0.0 copy-done.5
  1.6 0.0 copy-start
  1.6 1.1 %copy-done = f32[5,8,32,128]{3,2,1,0:T(8,128)S(1)} copy-done((f32[5,8,32,128]{3,2,1,0:T(8,128)S(1)}, f32[5,8,32,128]{3,2,1,0:T(8,128)}, u32[]{:S(2)}) %copy-start) | copy-done | bytes 655384
  2.6 0.0 copy-start.1
  2.6 1.1 %copy-done.1 = f32[5,8,32,128]{3,2,1,0:T(8,128)S(1)} copy-done((f32[5,8,32,128]{3,2,1,0:T(8,128)S(1)}, f32[5,8,32,128]{3,2,1,0:T(8,128)}, u32[]{:S(2)}) %copy-start.1) | copy-done | bytes 655384
  3.7 0.0 copy-start.2
  3.7 1.1 %copy-done.2 = f32[5,8,32,128]{3,2,1,0:T(8,128)S(1)} copy-done((f32[5,8,32,128]{3,2,1,0:T(8,128)S(1)}, f32[5,8,32,128]{3,2,1,0:T(8,128)}, u32[]{:S(2)}) %copy-start.2) | copy-done | bytes 655384
  4.8 0.0 copy-start.3
  4.8 1.0 %copy-done.3 = bf16[352,384]{1,0:T(8,128)(2,1)S(1)} copy-done((bf16[352,384]{1,0:T(8,128)(2,1)S(1)}, bf16[352,384]{1,0:T(8,128)(2,1)}, u32[]{:S(2)}) %copy-start.3) | copy-done | bytes 270360
  5.8 0.0 copy-start.4
  5.8 1.0 %copy-done.4 = f32[16,4224]{1,0:T(8,128)S(1)} copy-done((f32[16,4224]{1,0:T(8,128)S(1)}, f32[16,4224]{1,0:T(8,128)}, u32[]{:S(2)}) %copy-start.4) | copy-done | bytes 270360
  6.7 55.1 %shard_map.102 = (f32[5,8,32,128]{3,2,1,0:T(8,128)S(1)}, f32[5,4,16,128]{3,2,1,0:T(8,128)S(1)}, f32[5,2,8,128]{3,2,1,0:T(8,128)S(1)}, f32[5,1,4,128]{3,2,1,0:T(4,128)S(1)}) custom-call(f32[5,8,32,128]{3,2,1,0:T(8,128)S(1)} %copy-done, f32[5,8,32,128]{3,2,1,0:T(8,128)S(1)} %copy-done.1, f32[5,8,32,128]{3,2,1,0:T(8,128)S(1)} %copy-done.2, ...), custom_call_target="tpu_custom_call" | custom-call | tf_op jit(solution)/shard_map/pallas_call | solution.py:439
  61.8 0.8 %copy.16 = f32[5,8,32,128]{3,2,1,0:T(8,128)} copy(f32[5,8,32,128]{3,2,1,0:T(8,128)S(1)} %get-tuple-element.8) | data formatting | bytes 1310720
  62.7 0.7 %copy.17 = f32[5,4,16,128]{3,2,1,0:T(8,128)} copy(f32[5,4,16,128]{3,2,1,0:T(8,128)S(1)} %get-tuple-element.9) | data formatting | bytes 327680
  63.3 0.6 copy.18
  63.9 0.6 copy.19
Async XLA Ops:
  0.6 0.9 %copy-start.5 = (s32[8,32,128]{2,1,0:T(8,128)S(1)}, s32[8,32,128]{2,1,0:T(8,128)}, u32[]{:S(2)}) copy-start(s32[8,32,128]{2,1,0:T(8,128)} %refs_3_.1) | copy-start | bytes 393220
  1.6 1.1 %copy-start = (f32[5,8,32,128]{3,2,1,0:T(8,128)S(1)}, f32[5,8,32,128]{3,2,1,0:T(8,128)}, u32[]{:S(2)}) copy-start(f32[5,8,32,128]{3,2,1,0:T(8,128)} %refs_0_.1) | copy-start | bytes 1966084
  2.6 1.1 %copy-start.1 = (f32[5,8,32,128]{3,2,1,0:T(8,128)S(1)}, f32[5,8,32,128]{3,2,1,0:T(8,128)}, u32[]{:S(2)}) copy-start(f32[5,8,32,128]{3,2,1,0:T(8,128)} %refs_1_.1) | copy-start | bytes 1966084
  3.7 1.1 %copy-start.2 = (f32[5,8,32,128]{3,2,1,0:T(8,128)S(1)}, f32[5,8,32,128]{3,2,1,0:T(8,128)}, u32[]{:S(2)}) copy-start(f32[5,8,32,128]{3,2,1,0:T(8,128)} %refs_2_.1) | copy-start | bytes 1966084
  4.8 1.0 %copy-start.3 = (bf16[352,384]{1,0:T(8,128)(2,1)S(1)}, bf16[352,384]{1,0:T(8,128)(2,1)}, u32[]{:S(2)}) copy-start(bf16[352,384]{1,0:T(8,128)(2,1)} %constant.5.clone.refs_6_) | copy-start | bytes 811012
  5.8 1.0 %copy-start.4 = (f32[16,4224]{1,0:T(8,128)S(1)}, f32[16,4224]{1,0:T(8,128)}, u32[]{:S(2)}) copy-start(f32[16,4224]{1,0:T(8,128)} %constant.4.clone.refs_5_) | copy-start | bytes 811012
where the time goes:
time: 64.9 us; the launch traced here: 64.5 us
  Pallas kernels  55.1 us (85%)
  local copies, waits for them, and re-layouts  8.79 us (14%)
  between operations  0.67 us (1%)
    pallas_call x1, Pallas kernels, body(): pl.pallas_call(functools.partial(kernel, levels, count_x, count_y), out_s...  55.1 us
    unnamed x17, local copies, waits for them, and re-layouts  8.79 us

commit v1 on v0

--- a/solution.py
+++ b/solution.py
@@ -76,14 +76,20 @@
 def kernel(levels, count_x, count_y, *refs):
     refs = list(refs)
     take = lambda n: [refs.pop(0) for _ in range(n)]
-    guess_ref, right_ref, conduct_ref, mask_ref, stencil_ref, plan_ref, moves_ref = take(7)
+    stencil_ref = refs.pop(0)
+    sources, targets = take(6), take(4)
+    loaded = guess_ref, mask_ref, right_ref, conduct_ref, plan_ref, moves_ref = take(6)
     outs = take(4)
     weight = take(LEVELS)
     high, low = take(LEVELS), take(LEVELS)
     high2, low2 = take(LEVELS), take(LEVELS)
     conduct, share, force, ratio, gain, state = [take(LEVELS) for _ in range(6)]
     edge, side, side_out = [take(sum(ROUNDS)) for _ in range(3)]
-    send_sem, recv_sem = take(2)
+    send_sem, recv_sem, load_sem, store_sem = take(4)
+    loads = [pltpu.make_async_copy(a, b, load_sem.at[i]) for i, (a, b) in enumerate(zip(sources, loaded))]
+    stores = [pltpu.make_async_copy(a, b, store_sem.at[i]) for i, (a, b) in enumerate(zip(outs, targets))]
+    for load in loads:
+        load.start()
 
     at_x, at_y = lax.axis_index("gx"), lax.axis_index("gy")
 
@@ -178,13 +184,25 @@
                 y = b * lev.yp + lev.y - 1 - i
                 side_out[rnd][1, x, pl.ds(8 * i + b, 1), :] = values[y : y + 1]
 
-    def convert(l, rnd, x):
+    def convert_rows(l, x, first_row, values):
+        a, b = split(values)
+        high[l][x, pl.ds(first_row, values.shape[0]), :] = a
+        low[l][x, pl.ds(first_row, values.shape[0]), :] = b
+
+    def convert_plane(l, rnd, x):
+        convert_rows(l, x, 0, edge[rnd][x])
+
+    def convert_halo(l, rnd, x):
         lev = levels[l]
         halo = [side[rnd][i, x, pl.ds(k, 8), :] for k in range(0, lev.halo // 2, 8) for i in range(2)]
-        for start, values in ((0, edge[rnd][x]), (lev.rows, jnp.concatenate(halo, axis=0))):
-            a, b = split(values)
-            high[l][x, pl.ds(start, values.shape[0]), :] = a
-            low[l][x, pl.ds(start, values.shape[0]), :] = b
+        convert_rows(l, x, lev.rows, jnp.concatenate(halo, axis=0))
+
+    def convert_own(l, rnd):
+        start = width_of(rnd)
+        loop(start, start + levels[l].x, lambda x: convert_plane(l, rnd, x))
+
+    def loop(start, stop, step):
+        lax.fori_loop(start, stop, lambda i, _: (step(i), 0)[1], 0)
 
     def apply_group(l, x0, n, high_ref, low_ref):
         lev = levels[l]
@@ -215,12 +233,14 @@
                 store(2 * p + i, summed)
             return 0
 
+        convert_own(0, rnd)
         receive(0, rnd, FACES_Y)
-        lax.fori_loop(1, lev.x + 1, lambda x, _: (convert(0, rnd, x), 0)[1], 0)
+        loop(1, lev.x + 1, lambda x: convert_halo(0, rnd, x))
         lax.fori_loop(1, pairs - 1, pair, 0)
         receive(0, rnd, FACES_X)
-        convert(0, rnd, 0)
-        convert(0, rnd, lev.x + 1)
+        for x in (0, lev.x + 1):
+            convert_plane(0, rnd, x)
+            convert_halo(0, rnd, x)
         lax.fori_loop(0, 2, lambda p, _: pair(p * (pairs - 1), 0), 0)
 
     def build_weight(l):
@@ -327,11 +347,15 @@
         put(0, 0, x, s * guess_ref[:, x].reshape(fine.rows, 128))
         return 0
 
+    loads[0].wait()
+    loads[1].wait()
     lax.fori_loop(0, fine.x, start, 0)
     pl.semaphore_wait(barrier, neighbours)
     send(0, 0)
 
     scale = relax(fine)
+    for load in loads[2:]:
+        load.wait()
 
     def prepare(x, _):
         f = right_ref[:, x].reshape(fine.rows, 128)
@@ -340,10 +364,7 @@
         return 0
 
     lax.fori_loop(0, fine.x, prepare, 0)
-    for l in range(LEVELS - 1):
-        coarse_means(l)
-    for l in range(LEVELS):
-        build_weight(l)
+    build_weight(0)
     for l in range(1, LEVELS):
         for ref in (high2[l], low2[l]):
             ref[:, pl.ds(levels[l].out, 16), :] = jnp.zeros((levels[l].x + 2, 16, 128), BF16)
@@ -366,14 +387,26 @@
     for rnd, store in enumerate((first, second, third)):
         sweep_fine(rnd, store)
         send(0, rnd + 1)
+        if rnd == 0:
+            for l in range(LEVELS - 1):
+                coarse_means(l)
+        else:
+            build_weight(rnd)
+        if rnd == 1:
+            stores[0].start()
 
     for l in range(1, LEVELS):
         lev, base = levels[l], first_round[l]
         restrict(l - 1, base - 1)
+        if l == 1:
+            build_weight(LEVELS - 1)
 
         wide = 2 if lev.x > 1 else 3
+        convert_own(l, base + 1)
         receive(l, base + 1, ways(l, base + 1))
-        lax.fori_loop(0, lev.x + 4, lambda x, _, l=l, base=base: (convert(l, base + 1, x), 0)[1], 0)
+        for x in (0, 1, lev.x + 2, lev.x + 3):
+            convert_plane(l, base + 1, x)
+        loop(0, lev.x + 4, lambda x, l=l, base=base: convert_halo(l, base + 1, x))
         receive(l, base, FACES_Y + FACES_X)
 
         def smooth(p, _, l=l, lev=lev, base=base, wide=wide):
@@ -404,6 +437,8 @@
             return 0
 
         lax.fori_loop(0, (lev.x + 2) // wide, smooth, 0)
+        if l < LEVELS - 1:
+            stores[l].start()
         lax.fori_loop(0, max(1, lev.x // 2), remain, 0)
         if l < LEVELS - 1:
             send(l, base + 2)
@@ -411,6 +446,9 @@
     for l in range(LEVELS):
         for rnd in range(first_round[l], first_round[l] + ROUNDS[l]):
             finish(l, rnd)
+    stores[LEVELS - 1].start()
+    for store in stores:
+        store.wait()
 
 
 def body(count_x, count_y, initial_guess, right_side, coefficients, tunnel_mask, stencil):
@@ -423,10 +461,12 @@
     moves = [m for l in range(LEVELS - 1) for m in transfer_matrices(levels[l], levels[l + 1])]
     widest = -(-max(m.shape[1] for m in moves) // 128) * 128
     moves = np.concatenate([np.pad(m, ((0, 0), (0, widest - m.shape[1]))) for m in moves], axis=0)
-    operands = [initial_guess, right_side, coefficients, tunnel_mask, stencil]
+    operands = [stencil, initial_guess, tunnel_mask, right_side, coefficients]
     operands += [jnp.asarray(plan), jnp.asarray(moves, BF16)]
-    vmem = pl.BlockSpec(memory_space=pltpu.VMEM)
-    scratch = [pltpu.VMEM((3 * lev.out, lev.total), BF16) for lev in levels]
+    anywhere = pl.BlockSpec(memory_space=pl.ANY)
+    results = [jax.ShapeDtypeStruct((COMP, lev.x, lev.y, 128), F32) for lev in levels]
+    scratch = [pltpu.VMEM(held.shape, held.dtype) for held in operands[1:] + results]
+    scratch += [pltpu.VMEM((3 * lev.out, lev.total), BF16) for lev in levels]
     for extra in (4, 4, 2, 2):
         scratch += [pltpu.VMEM((lev.x + extra, lev.depth, 128), BF16) for lev in levels]
     for _ in range(6):
@@ -436,14 +476,15 @@
     scratch += [pltpu.VMEM((2, lev.x + 2 * width, 8 * width, 128), F32) for lev, width in of_round]
     scratch += [pltpu.VMEM((2, lev.x, 8 * width, 128), F32) for lev, width in of_round]
     scratch += [pltpu.SemaphoreType.DMA((len(of_round), len(ALL)))] * 2
+    scratch += [pltpu.SemaphoreType.DMA((6,)), pltpu.SemaphoreType.DMA((4,))]
     return pl.pallas_call(
         functools.partial(kernel, levels, count_x, count_y),
-        out_shape=[jax.ShapeDtypeStruct((COMP, lev.x, lev.y, 128), F32) for lev in levels],
-        in_specs=[vmem] * len(operands),
-        out_specs=[vmem] * 4,
+        out_shape=results,
+        in_specs=[pl.BlockSpec(memory_space=pltpu.VMEM)] + [anywhere] * 6,
+        out_specs=[anywhere] * 4,
         scratch_shapes=scratch,
         compiler_params=pltpu.CompilerParams(
-            collective_id=0, has_side_effects=True, vmem_limit_bytes=48 * 1024 * 1024
+            collective_id=0, has_side_effects=True, vmem_limit_bytes=60 * 1024 * 1024
         ),
     )(*operands)
 

time: 64.9 us -> 61.4 us (0.946)
  local copies, waits for them, and re-layouts: 8.79 us -> 5.63 us
    unnamed x17 -> x11, local copies, waits for them, and re-layouts: 8.79 us -> 5.63 us
where the time goes in v1:
time: 61.4 us; the launch traced here: 61.1 us
  Pallas kernels  54.8 us (89%)
  local copies, waits for them, and re-layouts  5.63 us (9%)
  between operations  0.65 us (1%)
    pallas_call x1, Pallas kernels, body(): pl.pallas_call(functools.partial(kernel, levels, count_x, count_y), out_s...  54.8 us
    unnamed x11, local copies, waits for them, and re-layouts  5.63 us

profile of v1, /device:TPU:4, one launch (start us, length us, event | category | flops | bytes accessed | tf_op | source)
XLA Modules:
  0.0 61.1 jit_solution(1470041555095991374)
XLA Ops:
  0.6 1.5 %copy.11.refs_0_ = f32[27,5,5]{2,1,0:T(8,128)} copy(f32[27,5,5]{0,2,1:T(8,128)} %param.11) | data formatting | bytes 5400 | tf_op args[4]
  2.1 54.8 %shard_map.102 = (f32[5,8,32,128]{3,2,1,0:T(8,128)}, f32[5,4,16,128]{3,2,1,0:T(8,128)}, f32[5,2,8,128]{3,2,1,0:T(8,128)}, f32[5,1,4,128]{3,2,1,0:T(4,128)}) custom-call(f32[27,5,5]{2,1,0:T(8,128)} %copy.11.refs_0_, f32[5,8,32,128]{3,2,1,0:T(8,128)} %refs_1_.1, s32[8,32,128]{2,1,0:T(8,128)} %refs_2_.1, f32[5,8,32,128]{3,2,1,0:T(8,128)} %refs_3_.1, ...), custom_call_target="tpu_custom_call" | custom-call | tf_op jit(solution)/shard_map/pallas_call | solution.py:480
  57.0 0.0 copy-start
  57.0 2.0 %copy.16 = f32[5,8,32,128]{3,2,1,0:T(8,128)} copy(f32[5,8,32,128]{3,2,1,0:T(8,128)} %get-tuple-element.8) | data formatting | bytes 1310720
  59.0 0.0 copy-done
  59.0 0.0 copy-start.1
  59.0 0.7 %copy.17 = f32[5,4,16,128]{3,2,1,0:T(8,128)} copy(f32[5,4,16,128]{3,2,1,0:T(8,128)S(1)} %copy-done) | data formatting | bytes 327680
  59.7 0.1 copy-done.1
  59.8 0.0 copy-start.2
  59.8 0.6 %copy.18 = f32[5,2,8,128]{3,2,1,0:T(8,128)} copy(f32[5,2,8,128]{3,2,1,0:T(8,128)S(1)} %copy-done.1) | data formatting | bytes 81920
  60.4 0.1 copy-done.2
  60.5 0.6 copy.19
Async XLA Ops:
  57.0 2.0 %copy-start = (f32[5,4,16,128]{3,2,1,0:T(8,128)S(1)}, f32[5,4,16,128]{3,2,1,0:T(8,128)}, u32[]{:S(2)}) copy-start(f32[5,4,16,128]{3,2,1,0:T(8,128)} %get-tuple-element.9) | copy-start | bytes 491524
  59.0 0.8 %copy-start.1 = (f32[5,2,8,128]{3,2,1,0:T(8,128)S(1)}, f32[5,2,8,128]{3,2,1,0:T(8,128)}, u32[]{:S(2)}) copy-start(f32[5,2,8,128]{3,2,1,0:T(8,128)} %get-tuple-element.10) | copy-start | bytes 122884
  59.8 0.7 %copy-start.2 = (f32[5,1,4,128]{3,2,1,0:T(4,128)S(1)}, f32[5,1,4,128]{3,2,1,0:T(4,128)}, u32[]{:S(2)}) copy-start(f32[5,1,4,128]{3,2,1,0:T(4,128)} %get-tuple-element.11) | copy-start | bytes 30724
